TPU v7x, 512 devices: a whole 4x4x16 slice. The times are simulated.
512 devices in a mesh: freq: 8 (over x, core), tile: 64 (over z, y).
Axes of the slice: x: 4, y: 4, z: 16, core: 2. Of those that a mesh axis runs over, the one named last changes fastest.
Arguments:
- left_basis: bfloat16 [16, 8192, 2, 1536], P('freq', 'tile'), may hold values from -0.078125 to 0.078125
- right_basis: bfloat16 [16, 8192, 2, 1536], P('freq', 'tile'), may hold values from -0.25 to 0.25
- start_model: float32 [16, 8192, 128], P('freq', 'tile'), may hold values from -3 to 3
- recorded: float32 [16, 8192, 128], P('freq', 'tile'), may hold values from -6 to 6
- tile_ranks: int32 [16, 16], replicated, may hold values from 16 to 96, as said below
- mute_start: int32 [8192, 64], P('tile'), may hold values from 0 to 127
- thresholds: float32 [64], replicated, may hold values from 0.05 to 0.5
Outputs:
- estimate: float32 [16, 8192, 128], P('freq', 'tile')
- misfit: float32 [16, 8192, 128], P('freq', 'tile')
Inputs may be any that keep to these rules, and one draw needn't show every extreme that they name: `tile_ranks`: some tile has rank 96 and some rank 16.
All inputs are finite; a program needn't handle non-finite values.
Results may differ from a plain program's by a relative error of at most 0.013.
Values may be sent and summed in bfloat16 or wider, within the bound.
A program may use at most 64 MiB of HBM per device.

v0:
```python
import math

import jax
import jax.numpy as jnp
from jax import lax
from jax.sharding import PartitionSpec as P

NT = 256
OUTER = 2


STEP_SIZE = 0.5


def phase_table(freq_count):
    sample_index = lax.iota(jnp.int32, NT)[:, None]
    bin_index = lax.iota(jnp.int32, freq_count)[None, :] + NT // 4
    phases = (sample_index * bin_index % NT).astype(jnp.float32) * (2.0 * math.pi / NT)
    return jnp.stack([jnp.cos(phases), -jnp.sin(phases)])


def partials(basis, vector, rank_mask):
    frames = basis.shape[0]
    sources = vector.shape[2] // 2
    inside, rank_slots = rank_mask.shape
    product = jnp.einsum("fnak,fnc->fakc", basis, vector, preferred_element_type=jnp.float32)
    real_part = product[:, 0, :, :sources] + product[:, 1, :, sources:]
    imag_part = product[:, 0, :, sources:] - product[:, 1, :, :sources]
    partial_value = jnp.concatenate([real_part, imag_part], 2).reshape(
        frames, inside, rank_slots, 2 * sources
    )
    partial_value = partial_value * rank_mask[None, :, :, None]
    return partial_value.astype(jnp.bfloat16)


def expand(basis, coefficient):
    frames, height, planes, columns = basis.shape
    inside, share_count, rank_slots, narrow = coefficient.shape[1:]
    blocks = basis.reshape(frames, height, planes, inside, rank_slots)
    product = jnp.einsum(
        "fnajk,fjqkw->fnaqw", blocks, coefficient, preferred_element_type=jnp.float32
    )
    product = product.reshape(frames, height, planes, share_count * narrow)
    sources = share_count * narrow // 2
    real_part = product[:, :, 0, :sources] - product[:, :, 1, sources:]
    imag_part = product[:, :, 0, sources:] + product[:, :, 1, :sources]
    return jnp.concatenate([real_part, imag_part], 2)


def shuffle(partial_value):
    frames, inside, rank_slots, columns = partial_value.shape
    tile_count = lax.axis_size("tile")
    group_size = tile_count // inside
    outgoing = jnp.broadcast_to(
        partial_value[:, :, None], (frames, inside, group_size, rank_slots, columns)
    )
    outgoing = outgoing.reshape(frames, tile_count, rank_slots, columns)
    incoming = lax.all_to_all(outgoing, "tile", split_axis=1, concat_axis=1, tiled=True)
    incoming = incoming.reshape(frames, inside, group_size, rank_slots, columns).astype(jnp.float32)
    return jnp.sum(incoming, 2).astype(jnp.bfloat16)[:, :, None]


def sparsify(estimate, mute_start, thresholds):
    spread = lax.all_to_all(
        estimate.astype(jnp.bfloat16), "freq", split_axis=1, concat_axis=0, tiled=True
    ).astype(estimate.dtype)
    freq_count, rows_here, columns = spread.shape
    sources = columns // 2
    wave_table = phase_table(freq_count)
    stacked = spread.reshape(freq_count, rows_here, 2, sources)
    series = jnp.einsum(
        "atk,knas->nst", wave_table, stacked, precision=lax.Precision.HIGHEST
    ) / math.sqrt(freq_count)
    window = lax.dynamic_slice_in_dim(mute_start, lax.axis_index("freq") * rows_here, rows_here, 0)
    sample_index = lax.iota(jnp.int32, NT)
    series = jnp.where(
        sample_index[None, None, :] >= window[:, :, None], series, jnp.zeros_like(series)
    )
    cutoff = thresholds[None, :, None]
    series = series - jnp.clip(series, -cutoff, cutoff)
    returned = jnp.einsum("nst,atk->knas", series, wave_table, precision=lax.Precision.HIGHEST) * (
        2.0 * math.sqrt(freq_count) / NT
    )
    returned = returned.reshape(freq_count, rows_here, columns)
    return lax.all_to_all(
        returned.astype(jnp.bfloat16), "freq", split_axis=0, concat_axis=1, tiled=True
    ).astype(returned.dtype)


def body(left_basis, right_basis, start_model, recorded, tile_ranks, mute_start, thresholds):
    tile_count = lax.axis_size("tile")
    inside = tile_ranks.shape[0]
    group_size = tile_count // inside
    tile_block = lax.axis_index("tile") // group_size
    levels = lax.iota(jnp.int32, left_basis.shape[3] // inside)
    column_ranks = lax.dynamic_slice_in_dim(tile_ranks, tile_block, 1, 1)
    row_ranks = lax.dynamic_slice_in_dim(tile_ranks, tile_block, 1, 0).reshape(inside, 1)
    right_mask = (levels[None, :] < column_ranks).astype(jnp.float32)
    left_mask = (levels[None, :] < row_ranks).astype(jnp.float32)
    model = start_model
    misfit = recorded
    for outer_step in range(OUTER):
        forward = shuffle(partials(right_basis, model.astype(jnp.bfloat16), right_mask))
        misfit = expand(left_basis, forward) - recorded
        adjoint = shuffle(partials(left_basis, misfit.astype(jnp.bfloat16), left_mask))
        model = model - STEP_SIZE * expand(right_basis, adjoint)
        model = sparsify(model, mute_start, thresholds)
    return (model, misfit)


def solution(mesh):
    return jax.shard_map(
        body,
        mesh=mesh,
        in_specs=(
            P("freq", "tile", None, None),
            P("freq", "tile", None, None),
            P("freq", "tile", None),
            P("freq", "tile", None),
            P(),
            P("tile", None),
            P(),
        ),
        out_specs=(P("freq", "tile", None), P("freq", "tile", None)),
        check_vma=False,
    )
```

profile of v0, /device:TPU:1, one launch (start us, length us, event | category | flops | bytes accessed | tf_op | source)
XLA Modules:
  0.0 716.9 jit_solution(524899450441515643)
XLA Ops:
  0.7 0.9 dynamic-slice_reduce_fusion
  1.7 3.7 copy.151
  6.0 1.4 slice_add_fusion.3
  7.4 1.5 add.105
  8.9 2.5 sub.83
  11.4 2.4 fusion
  13.8 1.7 copy.143
  15.5 2.4 broadcast_in_dim.8
  17.9 19.5 %all-to-all-start = ((bf16[2,64,96,128]{3,2,0,1:T(8,128)(2,1)}), bf16[2,64,96,128]{3,2,0,1:T(8,128)(2,1)}, u32[]{:S(2)}, u32[]{:S(2)}) async-start(bf16[2,64,96,128]{3,2,0,1:T(8,128)(2,1)} %bitcast.221), calls=%async_computation | async-start | bytes 6291456 | tf_op jit(solution)/shard_map/all_to_all | solution.py:58
  37.5 3.7 copy.144
  41.2 1.0 copy.148
  42.2 0.7 fusion.67
  43.0 134.5 %all-to-all-done = bf16[2,64,96,128]{3,2,0,1:T(8,128)(2,1)} async-done(((bf16[2,64,96,128]{3,2,0,1:T(8,128)(2,1)}), bf16[2,64,96,128]{3,2,0,1:T(8,128)(2,1)}, u32[]{:S(2)}, u32[]{:S(2)}) %all-to-all-start) | async-done | bytes 3145760 | tf_op jit(solution)/shard_map/all_to_all | solution.py:58
  177.6 2.4 bitcast_reduce_fusion.3
  181.1 1.4 slice_add_fusion.2
  182.4 2.5 add.110
  184.9 2.5 sub.89
  187.4 2.7 fusion.1
  190.1 2.4 copy.150
  192.5 3.5 broadcast_in_dim.9
  196.1 10.5 %all-to-all-start.1 = ((bf16[2,64,96,128]{3,2,0,1:T(8,128)(2,1)}), bf16[2,64,96,128]{3,2,0,1:T(8,128)(2,1)}, u32[]{:S(2)}, u32[]{:S(2)}) async-start(bf16[2,64,96,128]{3,2,0,1:T(8,128)(2,1)} %bitcast.220), calls=%async_computation.1 | async-start | bytes 6291456 | tf_op jit(solution)/shard_map/all_to_all | solution.py:58
  206.8 138.0 %all-to-all-done.1 = bf16[2,64,96,128]{3,2,0,1:T(8,128)(2,1)} async-done(((bf16[2,64,96,128]{3,2,0,1:T(8,128)(2,1)}), bf16[2,64,96,128]{3,2,0,1:T(8,128)(2,1)}, u32[]{:S(2)}, u32[]{:S(2)}) %all-to-all-start.1) | async-done | bytes 3145760 | tf_op jit(solution)/shard_map/all_to_all | solution.py:58
  344.8 2.4 bitcast_reduce_fusion.2
  347.8 0.8 copy.156
  348.5 12.1 %all-to-all-start.2 = ((bf16[2,128,128]{2,0,1:T(2,128)(2,1)}), bf16[2,128,128]{2,0,1:T(2,128)(2,1)S(1)}, u32[]{:S(2)}, u32[]{:S(2)}) async-start(bf16[2,128,128]{2,0,1:T(2,128)(2,1)} %copy.156), calls=%async_computation.2 | async-start | bytes 131072 | tf_op jit(solution)/shard_map/all_to_all | solution.py:64
  360.7 0.7 neg.17
  361.4 4.0 all-to-all-done.2
  366.2 2.2 fusion.11
  368.7 8.0 %all_to_all.77 = bf16[16,16,128]{2,1,0:T(8,128)(2,1)S(1)} all-to-all(bf16[16,16,128]{2,1,0:T(8,128)(2,1)S(1)} %convert_element_type.128), channel_id=1, replica_groups=mesh['freq'=8,'tile'=64] {'freq'}, dimensions={0} | all-to-all | bytes 131072 | tf_op jit(solution)/shard_map/all_to_all | solution.py:85
  377.4 1.1 slice_add_fusion.1
  378.5 1.5 add.114
  380.0 1.3 sub.95
  381.3 2.4 fusion.2
  383.7 1.7 copy.165
  385.4 0.8 broadcast_in_dim.10
  386.3 146.4 %all_to_all.78 = bf16[2,64,96,128]{3,2,0,1:T(8,128)(2,1)S(1)} all-to-all(bf16[2,64,96,128]{3,2,0,1:T(8,128)(2,1)S(1)} %bitcast.223), channel_id=1, replica_groups=mesh['freq'=8,'tile'=64] {'tile'}, dimensions={1} | all-to-all | bytes 6291456 | tf_op jit(solution)/shard_map/all_to_all | solution.py:58
  535.9 0.9 copy.171
  536.7 2.4 broadcast_in_dim.11
  539.1 9.5 %all-to-all-start.5 = ((bf16[2,64,96,128]{3,2,0,1:T(8,128)(2,1)}), bf16[2,64,96,128]{3,2,0,1:T(8,128)(2,1)S(1)}, u32[]{:S(2)}, u32[]{:S(2)}) async-start(bf16[2,64,96,128]{3,2,0,1:T(8,128)(2,1)} %bitcast.222), calls=%async_computation.5 | async-start | bytes 6291456 | tf_op jit(solution)/shard_map/all_to_all | solution.py:58
  548.6 4.9 copy.206
  553.7 133.8 %all-to-all-done.5 = bf16[2,64,96,128]{3,2,0,1:T(8,128)(2,1)S(1)} async-done(((bf16[2,64,96,128]{3,2,0,1:T(8,128)(2,1)}), bf16[2,64,96,128]{3,2,0,1:T(8,128)(2,1)S(1)}, u32[]{:S(2)}, u32[]{:S(2)}) %all-to-all-start.5) | async-done | bytes 3145760 | tf_op jit(solution)/shard_map/all_to_all | solution.py:58
  688.0 0.9 copy-done.2
  689.6 14.5 %all_to_all.79 = bf16[2,128,128]{2,0,1:T(2,128)(2,1)S(1)} all-to-all(bf16[2,128,128]{2,0,1:T(2,128)(2,1)S(1)} %copy.174), channel_id=1, replica_groups=mesh['freq'=8,'tile'=64] {'freq'}, dimensions={1} | all-to-all | bytes 131072 | tf_op jit(solution)/shard_map/all_to_all | solution.py:64
  704.8 1.6 fusion.10
  706.6 0.7 convert_element_type.136
  707.3 4.0 all-to-all-start.7
  711.4 0.8 copy.180
  712.1 4.1 all-to-all-done.7
  (68 shorter events, 10.3 us)
Async XLA Ops:
  0.6 360.0 %copy-start = (s32[128,64]{0,1:T(8,128)S(1)}, s32[128,64]{0,1:T(8,128)}, u32[]{:S(2)}) copy-start(s32[128,64]{0,1:T(8,128)} %param.12) | copy-start | bytes 98308
  0.6 4.8 copy-start.5
  1.7 9.7 %copy-start.6 = (f32[16,96]{1,0:T(8,128)}, f32[16,96]{1,0:T(8,128)S(1)}, u32[]{:S(2)}) copy-start(f32[16,96]{1,0:T(8,128)S(1)} %fusion.65) | copy-start | bytes 18436
  17.9 159.6 %all-to-all-start = ((bf16[2,64,96,128]{3,2,0,1:T(8,128)(2,1)}), bf16[2,64,96,128]{3,2,0,1:T(8,128)(2,1)}, u32[]{:S(2)}, u32[]{:S(2)}) async-start(bf16[2,64,96,128]{3,2,0,1:T(8,128)(2,1)} %bitcast.221), calls=%async_computation | async-start | bytes 6291456 | tf_op jit(solution)/shard_map/all_to_all | solution.py:58
  42.2 138.3 %copy-start.3 = (f32[2,128,128]{1,2,0:T(8,128)}, f32[2,128,128]{1,2,0:T(8,128)S(1)}, u32[]{:S(2)}) copy-start(f32[2,128,128]{1,2,0:T(8,128)S(1)} %copy.148) | copy-start | bytes 393220
  196.1 148.7 %all-to-all-start.1 = ((bf16[2,64,96,128]{3,2,0,1:T(8,128)(2,1)}), bf16[2,64,96,128]{3,2,0,1:T(8,128)(2,1)}, u32[]{:S(2)}, u32[]{:S(2)}) async-start(bf16[2,64,96,128]{3,2,0,1:T(8,128)(2,1)} %bitcast.220), calls=%async_computation.1 | async-start | bytes 6291456 | tf_op jit(solution)/shard_map/all_to_all | solution.py:58
  348.5 16.9 %all-to-all-start.2 = ((bf16[2,128,128]{2,0,1:T(2,128)(2,1)}), bf16[2,128,128]{2,0,1:T(2,128)(2,1)S(1)}, u32[]{:S(2)}, u32[]{:S(2)}) async-start(bf16[2,128,128]{2,0,1:T(2,128)(2,1)} %copy.156), calls=%async_computation.2 | async-start | bytes 131072 | tf_op jit(solution)/shard_map/all_to_all | solution.py:64
  361.4 15.9 %copy-start.9 = (f32[64]{0:T(128)}, f32[64]{0:T(128)S(1)}, u32[]{:S(2)}) copy-start(f32[64]{0:T(128)S(1)} %neg.17) | copy-start | bytes 772
  378.5 2.8 copy-start.7
  533.2 0.9 copy-start.4
  539.1 148.4 %all-to-all-start.5 = ((bf16[2,64,96,128]{3,2,0,1:T(8,128)(2,1)}), bf16[2,64,96,128]{3,2,0,1:T(8,128)(2,1)S(1)}, u32[]{:S(2)}, u32[]{:S(2)}) async-start(bf16[2,64,96,128]{3,2,0,1:T(8,128)(2,1)} %bitcast.222), calls=%async_computation.5 | async-start | bytes 6291456 | tf_op jit(solution)/shard_map/all_to_all | solution.py:58
  687.5 1.4 copy-start.2
  688.9 15.9 %copy-start.8 = (f32[64]{0:T(128)S(1)}, f32[64]{0:T(128)}, u32[]{:S(2)}) copy-start(f32[64]{0:T(128)} %param.13) | copy-start | bytes 772
  688.9 15.9 %copy-start.10 = (f32[64]{0:T(128)S(1)}, f32[64]{0:T(128)}, u32[]{:S(2)}) copy-start(f32[64]{0:T(128)} %copy-done.9) | copy-start | bytes 772
  689.5 27.4 %copy-start.1 = (s32[128,64]{0,1:T(8,128)S(1)}, s32[128,64]{0,1:T(8,128)}, u32[]{:S(2)}) copy-start(s32[128,64]{0,1:T(8,128)} %param.12) | copy-start | bytes 98308
  707.3 8.9 %all-to-all-start.7 = ((bf16[16,16,128]{2,1,0:T(8,128)(2,1)}), bf16[16,16,128]{2,1,0:T(8,128)(2,1)S(1)}, u32[]{:S(2)}, u32[]{:S(2)}) async-start(bf16[16,16,128]{2,1,0:T(8,128)(2,1)} %convert_element_type.136), calls=%async_computation.7 | async-start | bytes 131072 | tf_op jit(solution)/shard_map/all_to_all | solution.py:85
where the time goes:
time: 718 us; the launch traced here: 717 us
  waiting for transfers between devices  414 us (58%)
  blocking collectives  169 us (24%)
  starting transfers between devices  55.6 us (8%)
  local copies, waits for them, and re-layouts  48.7 us (7%)
  other arithmetic  18.9 us (3%)
  matrix products  9.25 us (1%)
    all_to_all x3, waiting for transfers between devices, shuffle(): lax.all_to_all(outgoing, 'tile', split_axis=1, concat_axis=1, tiled=True)  406 us
    all_to_all x1, blocking collectives, shuffle(): lax.all_to_all(outgoing, 'tile', split_axis=1, concat_axis=1, tiled=True)  146 us
    all_to_all x3, starting transfers between devices, shuffle(): lax.all_to_all(outgoing, 'tile', split_axis=1, concat_axis=1, tiled=True)  39.5 us
    all_to_all x1, blocking collectives, sparsify(): lax.all_to_all(estimate.astype(jnp.bfloat16), 'freq', split_axis=1, conca...  14.5 us
  transfers between devices with their start and end apart: 5, of which 5 were waited for; matrix products, arithmetic and copies ran while one was open for 2% of the time, Pallas kernels for 0%

commit v1 on v0

v1 whole, which is shorter than its diff:
```python
import math

import jax
import jax.numpy as jnp
import ml_dtypes
import numpy as np
from jax import lax
from jax.experimental import pallas as pl
from jax.experimental.pallas import tpu as pltpu
from jax.sharding import PartitionSpec as P

F32 = jnp.float32
BF16 = jnp.bfloat16
NT = 256
NF = 16
STEP_SIZE = 0.5


def split_table(table, terms):
    parts = []
    rest = table
    for _ in range(terms):
        part = rest.astype(ml_dtypes.bfloat16)
        parts.append(part)
        rest = rest - part.astype(np.float64)
    return parts


def wave_tables():
    sample = np.arange(NT)[:, None]
    bins = np.arange(NF)[None, :] + NT // 4
    phases = (sample * bins % NT) * (2.0 * math.pi / NT)
    table = np.concatenate([np.cos(phases), -np.sin(phases)], 1)
    forward = np.concatenate(split_table(table, 3), 1)
    backward = np.concatenate(split_table(np.ascontiguousarray(table.T), 2), 0)
    return forward, backward


def kernel(
    left, right, model0, recorded, ranks, mute, thresholds, wave, wave_back,
    estimate_out, misfit_out,
    left_rows, right_rows, left_cols, right_cols,
    model_full, model_half, recorded_half, packed, weights, product,
    outbox, inbox, own_sum, sib_sum, misfit_full,
    spread_out, spread_in, spread_f32, traces, traces_b, mute_rows,
    basis_s, basis_r, init_s, init_r, fwd_s, fwd_r, z_s, z_r, ex_s, ex_r,
    sp_s, sp_r, back_s, back_r, fin_s, fin_r, mis_s, mis_r,
):
    freq_id = lax.axis_index("freq")
    tile_id = lax.axis_index("tile")
    x, c = freq_id // 2, freq_id % 2
    z, y = tile_id // 4, tile_id % 4
    pair = z // 8
    me = (x, c, z, y)

    def address(place):
        return (place[0] * 2 + place[1], place[2] * 4 + place[3])

    def is_me(place):
        to = address(place)
        return jnp.logical_and(to[0] == freq_id, to[1] == tile_id)

    def remote(src, dst, send_sem, recv_sem, place):
        return pltpu.make_async_remote_copy(
            src_ref=src, dst_ref=dst, send_sem=send_sem, recv_sem=recv_sem,
            device_id=address(place), device_id_type=pl.DeviceIdType.MESH,
        )

    def send(src, dst, send_sem, recv_sem, place):
        mine = is_me(place)

        @pl.when(jnp.logical_not(mine))
        def _():
            remote(src, dst, send_sem, recv_sem, place).start()

        @pl.when(mine)
        def _():
            pltpu.make_async_copy(src, dst, recv_sem).start()

    def sent(src, dst, send_sem, recv_sem, place):
        @pl.when(jnp.logical_not(is_me(place)))
        def _():
            remote(src, dst, send_sem, recv_sem, place).wait_send()

    def arrived(ref, sem):
        pltpu.make_async_copy(ref, ref, sem).wait()

    barrier = pltpu.get_barrier_semaphore()

    def greet(place):
        pl.semaphore_signal(
            barrier, inc=1, device_id=address(place), device_id_type=pl.DeviceIdType.MESH
        )

    def greet_plane(index, carry):
        place = (index // 8, (index // 4) % 2, z, index % 4)

        @pl.when(jnp.logical_not(is_me(place)))
        def _():
            greet(place)
        return carry

    def greet_line(index, carry):
        @pl.when(8 * c + index != z)
        def _():
            greet((x, pair, 8 * c + index, y))
        return carry

    lax.fori_loop(0, 32, greet_plane, 0)
    lax.fori_loop(0, 8, greet_line, 0)
    pl.semaphore_wait(barrier, 39 - (pair == c).astype(jnp.int32))

    def basis_copy(which, t, q):
        source = (right, left)[which]
        rows = (right_rows, left_rows)[which]
        side, l = q // 2, q % 2
        return (
            source.at[l, :, 6 * side + t],
            rows.at[t, pl.ds(128 * y, 128)],
            basis_s.at[which, 4 * t + q],
            basis_r.at[which, t],
            (x, side, z, 2 * c + l),
        )

    def send_basis(which, t):
        def one(q, carry):
            send(*basis_copy(which, t, q))
            return carry
        lax.fori_loop(0, 4, one, 0)

    def init_copies(l):
        place = (x, y // 2, z, 2 * c + l)
        return (
            (model0.at[l], model_half.at[y % 2], init_s.at[l], init_r.at[0], place),
            (recorded.at[l], recorded_half.at[y % 2], init_s.at[2 + l], init_r.at[1], place),
        )

    for l in range(2):
        send(*init_copies(l)[0])
    for t in range(6):
        send_basis(0, t)
    for l in range(2):
        send(*init_copies(l)[1])

    sibling = (x, 1 - c, z, y)
    lane = lax.broadcasted_iota(jnp.int32, (1, 128), 1)
    low = lane < 64
    sign = jnp.where(low, 1.0, -1.0).astype(F32)

    mute_t = mute[...].astype(F32).T
    mute_rows[...] = jnp.concatenate([mute_t, mute_t], 1)
    first_row = pl.multiple_of(32 * x + 16 * c, 16)
    window = jnp.where(
        low, mute_rows[pl.ds(first_row, 8, stride=2), :], mute_rows[pl.ds(first_row + 1, 8, stride=2), :]
    )
    cutoff = jnp.concatenate([thresholds[...], thresholds[...]], 1)

    def set_weights(block, values):
        values = values.astype(BF16).astype(F32)
        packed[pl.ds(0, 128, stride=2), :] = values
        packed[pl.ds(1, 128, stride=2), :] = pltpu.roll(values, 64, 1) * sign
        weights[256 * block:256 * block + 256, :] = packed[...].astype(BF16)

    slots = lax.broadcasted_iota(jnp.int32, (96, 128), 0)

    def z_copy(step, s):
        return (
            outbox.at[step, s], inbox.at[step, z % 8], z_s.at[step, s], z_r.at[step, z % 8],
            (x, pair, 8 * c + s, y),
        )

    def partials(step, cols, h):
        values = jnp.dot(
            cols[384 * h:384 * h + 384, :], weights[...], preferred_element_type=F32
        )
        for s4 in range(4):
            s = 4 * h + s4
            other = 8 * c + s
            rank = ranks[other, z] if step % 2 == 0 else ranks[z, other]
            part = values[96 * s4:96 * s4 + 96, :]
            outbox[step, s] = jnp.where(slots < rank, part, 0.0).astype(BF16)
            send(*z_copy(step, s))

    def transpose(rows, cols, t):
        cols[128 * t:128 * t + 128, :] = rows.reshape(6, 1024, 128)[t].T

    def expand(rows, step, block):
        start = 256 * block if isinstance(block, int) else pl.multiple_of(256 * block, 256)
        view = rows.reshape(6, 1024, 128)
        lhs = jnp.concatenate([view[t, pl.ds(start, 256), :] for t in range(6)], 1)
        rhs = inbox[step].reshape(768, 128)
        product[...] = jnp.dot(lhs, rhs, preferred_element_type=F32)
        real = product[pl.ds(0, 128, stride=2), :]
        imag = product[pl.ds(1, 128, stride=2), :]
        return real - pltpu.roll(imag, 64, 1) * sign

    def exchange(step, block, slot):
        return remote(
            own_sum.at[step, block], sib_sum.at[step, slot], ex_s.at[step, slot],
            ex_r.at[step, slot], sibling,
        )

    def receive_line(step):
        for s in range(8):
            arrived(inbox.at[step, s], z_r.at[step, s])

    def residual(step):
        receive_line(step)
        for block in range(4):
            part = expand(left_rows, step, block)
            kept = jnp.where(block // 2 == c, recorded_half[block % 2], 0.0)
            own_sum[step, block] = part - kept
            exchange(step, block, block).start()
        for block in range(4):
            exchange(step, block, block).wait_recv()
            values = own_sum[step, block] + sib_sum[step, block]
            if step == 2:
                misfit_full[block] = values
            set_weights(block, values)

    def update(step):
        receive_line(step)
        for q in range(2):
            block = 2 * (1 - c) + q
            own_sum[step, block] = expand(right_rows, step, block)
            exchange(step, block, q).start()
        for q in range(2):
            own_sum[step, 2 * c + q] = expand(right_rows, step, 2 * c + q)
        for q in range(2):
            exchange(step, 2 * (1 - c) + q, q).wait_recv()
            total = own_sum[step, 2 * c + q] + sib_sum[step, q]
            model_half[q] = model_half[q] - STEP_SIZE * total

    def spread_copy(outer, index):
        q, column, core = index // 8, (index // 2) % 4, index % 2
        return (
            spread_out.at[outer, q, pl.ds(pl.multiple_of(32 * column + 16 * core, 16), 16)],
            spread_in.at[outer, 4 * x + y],
            sp_s.at[outer, index], sp_r.at[outer],
            (column, core, z, 2 * c + q),
        )

    def sparsify(outer):
        spread_out[outer] = model_half[...].astype(BF16)

        def one(index, carry):
            send(*spread_copy(outer, index))
            return carry
        lax.fori_loop(0, 16, one, 0)
        arrived(spread_in.at[outer], sp_r.at[outer])
        spread_f32[...] = spread_in[outer].reshape(256, 128).astype(F32)
        flat = traces.reshape(256, 128)
        sample = lax.broadcasted_iota(jnp.int32, (NT, 128), 0).astype(F32)
        for p in range(8):
            even = spread_f32[pl.ds(2 * p, 16, stride=16), :]
            odd = spread_f32[pl.ds(2 * p + 1, 16, stride=16), :]
            real = jnp.where(low, even, pltpu.roll(odd, 64, 1))
            imag = jnp.where(low, pltpu.roll(even, 64, 1), odd)
            both = jnp.concatenate([real, imag], 0).astype(BF16)
            series = jnp.dot(
                wave[...], jnp.concatenate([both, both, both], 0), preferred_element_type=F32
            ) * (1.0 / math.sqrt(NF))
            series = jnp.where(sample >= window[p:p + 1, :], series, 0.0)
            series = series - jnp.clip(series, -cutoff, cutoff)
            high = series.astype(BF16)
            rest = (series - high.astype(F32)).astype(BF16)
            first = jnp.dot(wave_back[...], high, preferred_element_type=F32)
            second = jnp.dot(wave_back[0:32, :], rest, preferred_element_type=F32)
            returned = (first[0:32] + first[32:64] + second) * (2.0 * math.sqrt(NF) / NT)
            real, imag = returned[0:16], returned[16:32]
            flat[pl.ds(2 * p, 16, stride=16), :] = jnp.where(low, real, pltpu.roll(imag, 64, 1))
            flat[pl.ds(2 * p + 1, 16, stride=16), :] = jnp.where(low, pltpu.roll(real, 64, 1), imag)

    def back_copy(index):
        owner, core = index // 2, index % 2
        return (
            traces_b.at[owner],
            model_full.at[pl.ds(pl.multiple_of(128 * y + 32 * x + 16 * c, 16), 16)],
            back_s.at[index], back_r.at[0],
            (owner // 4, core, z, owner % 4),
        )

    def final_copy(index):
        return (
            traces.at[pl.ds(2 * index, 2)],
            estimate_out.at[:, pl.ds(pl.multiple_of(32 * x + 16 * c, 16), 16)],
            fin_s.at[index], fin_r.at[0],
            (index // 2, index % 2, z, y),
        )

    def misfit_copy(q):
        return (
            misfit_full.at[2 * c + q], misfit_out.at[y % 2], mis_s.at[q], mis_r.at[0],
            (x, y // 2, z, 2 * c + q),
        )

    arrived(model_half, init_r.at[0])
    forward = remote(model_half, sib_sum.at[3, pl.ds(2, 2)], fwd_s.at[0], fwd_r.at[0], sibling)
    forward.start()
    forward.wait_recv()
    for block in range(4):
        mine = model_half[block % 2]
        theirs = sib_sum[3, 2 + block % 2]
        set_weights(block, jnp.where(block // 2 == c, mine, theirs))

    for t in range(6):
        arrived(right_rows.at[t], basis_r.at[0, t])
        send_basis(1, t)
        transpose(right_rows, right_cols, t)
        if t % 3 == 2:
            partials(0, right_cols, t // 3)
    for t in range(6):
        arrived(left_rows.at[t], basis_r.at[1, t])
        transpose(left_rows, left_cols, t)
    arrived(recorded_half, init_r.at[1])
    forward.wait_send()

    for outer in range(2):
        if outer == 1:
            partials(2, right_cols, 0)
            partials(2, right_cols, 1)
        residual(2 * outer)
        partials(2 * outer + 1, left_cols, 0)
        partials(2 * outer + 1, left_cols, 1)
        if outer == 1:
            for q in range(2):
                send(*misfit_copy(q))
        update(2 * outer + 1)
        sparsify(outer)
        if outer == 0:
            traces_b[...] = traces[...].astype(BF16)

            def back_one(index, carry):
                send(*back_copy(index))
                return carry
            lax.fori_loop(0, 32, back_one, 0)
            arrived(model_full, back_r.at[0])
            for block in range(4):
                set_weights(block, model_full[128 * block:128 * block + 128, :].astype(F32))
            for q in range(2):
                rows = pl.ds(pl.multiple_of(256 * c + 128 * q, 128), 128)
                model_half[q] = model_full[rows, :].astype(F32)

    def final_one(index, carry):
        send(*final_copy(index))
        return carry
    lax.fori_loop(0, 8, final_one, 0)

    def basis_done(index, carry):
        for which in range(2):
            sent(*basis_copy(which, index // 4, index % 4))
        return carry
    lax.fori_loop(0, 24, basis_done, 0)
    for l in range(2):
        for item in init_copies(l):
            sent(*item)
        sent(*misfit_copy(l))
    for step in range(4):
        def z_done(s, carry):
            sent(*z_copy(step, s))
            return carry
        lax.fori_loop(0, 8, z_done, 0)
        if step % 2 == 0:
            for block in range(4):
                exchange(step, block, block).wait_send()
        else:
            for q in range(2):
                exchange(step, 2 * (1 - c) + q, q).wait_send()

    def spread_done(index, carry):
        for outer in range(2):
            sent(*spread_copy(outer, index))
        return carry
    lax.fori_loop(0, 16, spread_done, 0)

    def back_done(index, carry):
        sent(*back_copy(index))
        return carry
    lax.fori_loop(0, 32, back_done, 0)

    def final_done(index, carry):
        sent(*final_copy(index))
        return carry
    lax.fori_loop(0, 8, final_done, 0)
    arrived(misfit_out, mis_r.at[0])
    arrived(estimate_out, fin_r.at[0])


def body(left_basis, right_basis, start_model, recorded, tile_ranks, mute_start, thresholds):
    def lanes(basis):
        return basis.reshape(2, 128, 2, 12, 128).transpose(0, 1, 3, 2, 4)

    wave, wave_back = wave_tables()
    anywhere = pl.BlockSpec(memory_space=pl.ANY)
    vmem = pl.BlockSpec(memory_space=pltpu.VMEM)
    dma = pltpu.SemaphoreType.DMA
    field = jax.ShapeDtypeStruct((2, 128, 128), F32)
    return pl.pallas_call(
        kernel,
        out_shape=(field, field),
        in_specs=[anywhere] * 4 + [pl.BlockSpec(memory_space=pltpu.SMEM)] + [vmem] * 4,
        out_specs=(vmem, vmem),
        scratch_shapes=[
            pltpu.VMEM((6, 512, 2, 128), BF16),
            pltpu.VMEM((6, 512, 2, 128), BF16),
            pltpu.VMEM((768, 1024), BF16),
            pltpu.VMEM((768, 1024), BF16),
            pltpu.VMEM((512, 128), BF16),
            pltpu.VMEM((2, 128, 128), F32),
            pltpu.VMEM((2, 128, 128), F32),
            pltpu.VMEM((256, 128), F32),
            pltpu.VMEM((1024, 128), BF16),
            pltpu.VMEM((256, 128), F32),
            pltpu.VMEM((4, 8, 96, 128), BF16),
            pltpu.VMEM((4, 8, 96, 128), BF16),
            pltpu.VMEM((4, 4, 128, 128), F32),
            pltpu.VMEM((4, 4, 128, 128), F32),
            pltpu.VMEM((4, 128, 128), F32),
            pltpu.VMEM((2, 2, 128, 128), BF16),
            pltpu.VMEM((2, 16, 16, 128), BF16),
            pltpu.VMEM((256, 128), F32),
            pltpu.VMEM((16, 16, 128), F32),
            pltpu.VMEM((16, 16, 128), BF16),
            pltpu.VMEM((128, 128), F32),
            dma((2, 24)), dma((2, 6)), dma((4,)), dma((2,)), dma((1,)), dma((1,)),
            dma((4, 8)), dma((4, 8)), dma((4, 4)), dma((4, 4)),
            dma((2, 16)), dma((2,)), dma((32,)), dma((1,)), dma((8,)), dma((1,)), dma((2,)), dma((1,)),
        ],
        compiler_params=pltpu.CompilerParams(
            collective_id=0, has_side_effects=True, vmem_limit_bytes=40 * 1024 * 1024
        ),
    )(
        lanes(left_basis), lanes(right_basis), start_model, recorded, tile_ranks,
        mute_start.T, thresholds.reshape(1, 64), jnp.asarray(wave), jnp.asarray(wave_back),
    )


def solution(mesh):
    return jax.shard_map(
        body,
        mesh=mesh,
        in_specs=(
            P("freq", "tile", None, None),
            P("freq", "tile", None, None),
            P("freq", "tile", None),
            P("freq", "tile", None),
            P(),
            P("tile", None),
            P(),
        ),
        out_specs=(P("freq", "tile", None), P("freq", "tile", None)),
        check_vma=False,
    )
```

time: 718 us -> 137 us (0.19)
  waiting for transfers between devices: 414 us -> 0 us
  blocking collectives: 169 us -> 0 us
  Pallas kernels: 0 us -> 126 us
  starting transfers between devices: 55.6 us -> 0 us
  local copies, waits for them, and re-layouts: 48.7 us -> 9.63 us
  other arithmetic: 18.9 us -> 0 us
  matrix products: 9.25 us -> 0 us
    all_to_all x5 -> x0, waiting for transfers between devices: 414 us -> none  [the longest x3 406 us: shuffle(): lax.all_to_all(outgoing, 'tile', split_axis=1, concat_axis=1, tiled=True)]
    all_to_all x3 -> x0, blocking collectives: 169 us -> none  [the longest x1 146 us: shuffle(): lax.all_to_all(outgoing, 'tile', split_axis=1, concat_axis=1, tiled=True)]
    pallas_call x0 -> x1, Pallas kernels: none -> 126 us  [body(): pl.pallas_call(kernel, out_shape=(field, field), in_specs=[anywhere] * 4...]
    all_to_all x5 -> x0, starting transfers between devices: 55.6 us -> none  [the longest x3 39.5 us: shuffle(): lax.all_to_all(outgoing, 'tile', split_axis=1, concat_axis=1, tiled=True)]
    convert_element_type x11 -> x0, local copies, waits for them, and re-layouts: 9.35 us -> none  [the longest x4 6.67 us: partials(): return partial_value.astype(jnp.bfloat16)]
    dot_general x12 -> x0, matrix products: 9.25 us -> none  [the longest x2 3.8 us: sparsify(): jnp.einsum('nst,atk->knas', series, wave_table, precision=lax.Precision.H...]
    broadcast_in_dim x4 -> x0, local copies, waits for them, and re-layouts: 9.16 us -> none  [shuffle(): jnp.broadcast_to(partial_value[:, :, None], (frames, inside, group_size,...]
    convert_element_type x9 -> x0, other arithmetic: 8.01 us -> none  [the longest x4 7.81 us: partials(): return partial_value.astype(jnp.bfloat16)]
  transfers between devices with their start and end apart: 5 -> 0, of which waited for: 5 -> 0; matrix products, arithmetic and copies ran while one was open for 2% -> 0% of each run, Pallas kernels for 0% -> 0%
where the time goes in v1:
time: 137 us; the launch traced here: 136 us
  Pallas kernels  126 us (92%)
  local copies, waits for them, and re-layouts  9.63 us (7%)
    pallas_call x1, Pallas kernels, body(): pl.pallas_call(kernel, out_shape=(field, field), in_specs=[anywhere] * 4...  126 us
    unnamed x20, local copies, waits for them, and re-layouts  9.63 us

profile of v1, /device:TPU:1, one launch (start us, length us, event | category | flops | bytes accessed | tf_op | source)
XLA Modules:
  0.0 136.2 jit_solution(2564237127842550102)
XLA Ops:
  0.6 0.0 copy-start
  0.6 1.4 %copy-done = bf16[2,128,2,1536]{3,2,1,0:T(2,128)(2,1)S(1)} copy-done((bf16[2,128,2,1536]{3,2,1,0:T(2,128)(2,1)S(1)}, bf16[2,128,2,1536]{3,2,1,0:T(2,128)(2,1)}, u32[]{:S(2)}) %copy-start) | copy-done | bytes 1572888
  2.0 0.0 copy-start.1
  2.0 1.4 %copy-done.1 = bf16[2,128,2,1536]{3,2,1,0:T(2,128)(2,1)S(1)} copy-done((bf16[2,128,2,1536]{3,2,1,0:T(2,128)(2,1)S(1)}, bf16[2,128,2,1536]{3,2,1,0:T(2,128)(2,1)}, u32[]{:S(2)}) %copy-start.1) | copy-done | bytes 1572888
  3.4 0.0 copy-start.2
  3.5 0.9 copy-done.2
  4.4 0.0 copy-start.3
  4.4 0.9 copy-done.3
  5.3 0.0 copy-start.4
  5.3 0.8 copy-done.4
  6.1 0.0 copy-start.5
  6.1 0.8 copy-done.5
  6.9 0.0 copy-start.6
  6.9 0.8 copy-done.6
  7.6 0.0 copy-start.7
  7.6 0.7 copy-done.7
  8.3 0.0 copy-start.8
  8.3 0.7 copy-done.8
  9.0 125.9 %shard_map.104 = (f32[2,128,128]{2,1,0:T(8,128)S(1)}, f32[2,128,128]{2,1,0:T(8,128)S(1)}) custom-call(bf16[2,128,12,2,128]{4,3,2,1,0:T(2,128)(2,1)S(1)} %bitcast.8, bf16[2,128,12,2,128]{4,3,2,1,0:T(2,128)(2,1)S(1)} %bitcast.9, f32[2,128,128]{2,1,0:T(8,128)S(1)} %copy-done.2, f32[2,128,128]{2,1,0:T(8,128)S(1)} %copy-done.3, s32[16,16]{1,0:T(8,128)S(1)} %copy-done.7, ...), custom_call_target="tpu_custom_call" | custom-call | tf_op jit(solution)/shard_map/pallas_call | solution.py:398
  134.9 0.7 copy.13
  135.5 0.7 copy.14
Async XLA Ops:
  0.6 1.4 %copy-start = (bf16[2,128,2,1536]{3,2,1,0:T(2,128)(2,1)S(1)}, bf16[2,128,2,1536]{3,2,1,0:T(2,128)(2,1)}, u32[]{:S(2)}) copy-start(bf16[2,128,2,1536]{3,2,1,0:T(2,128)(2,1)} %param.9) | copy-start | bytes 4718596
  2.0 1.4 %copy-start.1 = (bf16[2,128,2,1536]{3,2,1,0:T(2,128)(2,1)S(1)}, bf16[2,128,2,1536]{3,2,1,0:T(2,128)(2,1)}, u32[]{:S(2)}) copy-start(bf16[2,128,2,1536]{3,2,1,0:T(2,128)(2,1)} %param.10) | copy-start | bytes 4718596
  3.4 0.9 copy-start.2
  4.4 0.9 copy-start.3
  5.3 0.8 copy-start.4
  6.1 0.8 copy-start.5
  6.9 0.8 copy-start.6
  7.6 0.7 copy-start.7
  8.3 0.7 copy-start.8

commit v2 on v1

--- a/solution.py
+++ b/solution.py
@@ -14,6 +14,10 @@
 NT = 256
 NF = 16
 STEP_SIZE = 0.5
+PLANE = sorted(
+    ((dx, dy) for dx in range(4) for dy in range(4)),
+    key=lambda o: (-min(o[0], 4 - o[0]) - min(o[1], 4 - o[1]), o),
+)
 
 
 def split_table(table, terms):
@@ -37,13 +41,15 @@
 
 
 def kernel(
-    left, right, model0, recorded, ranks, mute, thresholds, wave, wave_back,
+    left, right, model0, recorded, ranks, mute_in, thresholds_in, wave_in, wave_back_in,
     estimate_out, misfit_out,
     left_rows, right_rows, left_cols, right_cols,
     model_full, model_half, recorded_half, packed, weights, product,
     outbox, inbox, own_sum, sib_sum, misfit_full,
     spread_out, spread_in, spread_f32, traces, traces_b, mute_rows,
-    basis_s, basis_r, init_s, init_r, fwd_s, fwd_r, z_s, z_r, ex_s, ex_r,
+    mute, thresholds, wave, wave_back, small_s,
+    local_rows, local_model, local_weights, group_out, group_in, local_r, group_s, group_r,
+    basis_s, basis_r, init_s, init_r, z_s, z_r, ex_s, ex_r,
     sp_s, sp_r, back_s, back_r, fin_s, fin_r, mis_s, mis_r,
 ):
     freq_id = lax.axis_index("freq")
@@ -66,7 +72,10 @@
             device_id=address(place), device_id_type=pl.DeviceIdType.MESH,
         )
 
-    def send(src, dst, send_sem, recv_sem, place):
+    def send(src, dst, send_sem, recv_sem, place, may_be_me=True):
+        if not may_be_me:
+            remote(src, dst, send_sem, recv_sem, place).start()
+            return
         mine = is_me(place)
 
         @pl.when(jnp.logical_not(mine))
@@ -77,7 +86,11 @@
         def _():
             pltpu.make_async_copy(src, dst, recv_sem).start()
 
-    def sent(src, dst, send_sem, recv_sem, place):
+    def sent(src, dst, send_sem, recv_sem, place, may_be_me=True):
+        if not may_be_me:
+            remote(src, dst, send_sem, recv_sem, place).wait_send()
+            return
+
         @pl.when(jnp.logical_not(is_me(place)))
         def _():
             remote(src, dst, send_sem, recv_sem, place).wait_send()
@@ -92,13 +105,12 @@
             barrier, inc=1, device_id=address(place), device_id_type=pl.DeviceIdType.MESH
         )
 
-    def greet_plane(index, carry):
-        place = (index // 8, (index // 4) % 2, z, index % 4)
-
-        @pl.when(jnp.logical_not(is_me(place)))
-        def _():
-            greet(place)
-        return carry
+    small = [
+        pltpu.make_async_copy(src, dst, small_s.at[i])
+        for i, (src, dst) in enumerate(
+            ((mute_in, mute), (thresholds_in, thresholds), (wave_in, wave), (wave_back_in, wave_back))
+        )
+    ]
 
     def greet_line(index, carry):
         @pl.when(8 * c + index != z)
@@ -106,9 +118,27 @@
             greet((x, pair, 8 * c + index, y))
         return carry
 
-    lax.fori_loop(0, 32, greet_plane, 0)
+    local_model_copy = pltpu.make_async_copy(model0, local_model, local_r.at[4])
+    local_model_copy.start()
+
+    def local_load(h):
+        for l in range(2):
+            for side in range(2):
+                for t3 in range(3):
+                    t = 6 * side + 3 * h + t3
+                    pltpu.make_async_copy(
+                        right.at[l, :, t], local_rows.at[l, 3 * (2 * h + side) + t3], local_r.at[2 * h + l]
+                    ).start()
+
+    local_load(0)
+    local_load(1)
     lax.fori_loop(0, 8, greet_line, 0)
-    pl.semaphore_wait(barrier, 39 - (pair == c).astype(jnp.int32))
+    for dx, dy in PLANE:
+        for dc in (1, 0):
+            if (dx, dy, dc) != (0, 0, 0):
+                greet(((x + dx) % 4, (c + dc) % 2, z, (y + dy) % 4))
+    for copy in small:
+        copy.start()
 
     def basis_copy(which, t, q):
         source = (right, left)[which]
@@ -135,31 +165,19 @@
             (recorded.at[l], recorded_half.at[y % 2], init_s.at[2 + l], init_r.at[1], place),
         )
 
-    for l in range(2):
-        send(*init_copies(l)[0])
-    for t in range(6):
-        send_basis(0, t)
-    for l in range(2):
-        send(*init_copies(l)[1])
-
     sibling = (x, 1 - c, z, y)
     lane = lax.broadcasted_iota(jnp.int32, (1, 128), 1)
     low = lane < 64
     sign = jnp.where(low, 1.0, -1.0).astype(F32)
 
-    mute_t = mute[...].astype(F32).T
-    mute_rows[...] = jnp.concatenate([mute_t, mute_t], 1)
-    first_row = pl.multiple_of(32 * x + 16 * c, 16)
-    window = jnp.where(
-        low, mute_rows[pl.ds(first_row, 8, stride=2), :], mute_rows[pl.ds(first_row + 1, 8, stride=2), :]
-    )
-    cutoff = jnp.concatenate([thresholds[...], thresholds[...]], 1)
-
-    def set_weights(block, values):
+    def interleave(values):
         values = values.astype(BF16).astype(F32)
         packed[pl.ds(0, 128, stride=2), :] = values
         packed[pl.ds(1, 128, stride=2), :] = pltpu.roll(values, 64, 1) * sign
-        weights[256 * block:256 * block + 256, :] = packed[...].astype(BF16)
+        return packed[...].astype(BF16)
+
+    def set_weights(block, values):
+        weights[256 * block:256 * block + 256, :] = interleave(values)
 
     slots = lax.broadcasted_iota(jnp.int32, (96, 128), 0)
 
@@ -169,17 +187,54 @@
             (x, pair, 8 * c + s, y),
         )
 
-    def partials(step, cols, h):
-        values = jnp.dot(
-            cols[384 * h:384 * h + 384, :], weights[...], preferred_element_type=F32
-        )
+    def fill_outbox(step, h, values):
         for s4 in range(4):
             s = 4 * h + s4
             other = 8 * c + s
             rank = ranks[other, z] if step % 2 == 0 else ranks[z, other]
             part = values[96 * s4:96 * s4 + 96, :]
             outbox[step, s] = jnp.where(slots < rank, part, 0.0).astype(BF16)
-            send(*z_copy(step, s))
+            if step == 0:
+                send(*z_copy(step, s))
+
+    def partials(step, cols, h):
+        fill_outbox(
+            step, h,
+            jnp.dot(cols[384 * h:384 * h + 384, :], weights[...], preferred_element_type=F32),
+        )
+
+    def group_copy(index):
+        h, l, side = index // 4, (index // 2) % 2, index % 2
+        return (
+            group_out.at[h, l, side], group_in.at[h, y], group_s.at[index], group_r.at[h],
+            (x, side, z, 2 * c + l),
+        )
+
+    def group_partials(h):
+        for l in range(2):
+            arrived(local_rows.at[l, pl.ds(6 * h, 6)], local_r.at[2 * h + l])
+            if h == 0:
+                local_weights[l] = interleave(local_model[l])
+            view = local_rows.reshape(2, 12, 256, 128)
+            for side in range(2):
+                for t3 in range(3):
+                    group_out[h, l, side, 128 * t3:128 * t3 + 128, :] = lax.dot_general(
+                        view[l, 3 * (2 * h + side) + t3], local_weights[l],
+                        (((0,), (0,)), ((), ())), preferred_element_type=F32,
+                    ).astype(BF16)
+
+    def send_line(step):
+        place = z % 8
+        upper = place // 4
+        reach = upper * (7 - place) + (1 - upper) * place
+        same = 1 - (pair + c) % 2
+        for k in range(8):
+            n = k + same * (7 - 2 * k)
+            inside = (2 * reach - n + 8) // 8
+            both = ((n + 1) // 2) * (2 * (n % 2) - 1)
+            one = (n - reach) * (1 - 2 * upper)
+            s = place + inside * both + (1 - inside) * one
+            send(*z_copy(step, s), may_be_me=k == 7)
 
     def transpose(rows, cols, t):
         cols[128 * t:128 * t + 128, :] = rows.reshape(6, 1024, 128)[t].T
@@ -231,8 +286,11 @@
             total = own_sum[step, 2 * c + q] + sib_sum[step, q]
             model_half[q] = model_half[q] - STEP_SIZE * total
 
+    SPREAD = [(dx, dc, q) for dx in (2, 1, 3, 0) for dc in (1, 0) for q in range(2)]
+
     def spread_copy(outer, index):
-        q, column, core = index // 8, (index // 2) % 4, index % 2
+        dx, dc, q = SPREAD[index]
+        column, core = (x + dx) % 4, (c + dc) % 2
         return (
             spread_out.at[outer, q, pl.ds(pl.multiple_of(32 * column + 16 * core, 16), 16)],
             spread_in.at[outer, 4 * x + y],
@@ -243,10 +301,8 @@
     def sparsify(outer):
         spread_out[outer] = model_half[...].astype(BF16)
 
-        def one(index, carry):
-            send(*spread_copy(outer, index))
-            return carry
-        lax.fori_loop(0, 16, one, 0)
+        for index in range(16):
+            send(*spread_copy(outer, index), may_be_me=index >= 14)
         arrived(spread_in.at[outer], sp_r.at[outer])
         spread_f32[...] = spread_in[outer].reshape(256, 128).astype(F32)
         flat = traces.reshape(256, 128)
@@ -271,13 +327,16 @@
             flat[pl.ds(2 * p, 16, stride=16), :] = jnp.where(low, real, pltpu.roll(imag, 64, 1))
             flat[pl.ds(2 * p + 1, 16, stride=16), :] = jnp.where(low, pltpu.roll(real, 64, 1), imag)
 
+    BACK = [(dx, dy, dc) for dx, dy in PLANE for dc in (1, 0)]
+
     def back_copy(index):
-        owner, core = index // 2, index % 2
-        return (
-            traces_b.at[owner],
+        dx, dy, dc = BACK[index]
+        column, row, core = (x + dx) % 4, (y + dy) % 4, (c + dc) % 2
+        return (
+            traces_b.at[4 * column + row],
             model_full.at[pl.ds(pl.multiple_of(128 * y + 32 * x + 16 * c, 16), 16)],
             back_s.at[index], back_r.at[0],
-            (owner // 4, core, z, owner % 4),
+            (column, core, z, row),
         )
 
     def final_copy(index):
@@ -294,46 +353,69 @@
             (x, y // 2, z, 2 * c + q),
         )
 
-    arrived(model_half, init_r.at[0])
-    forward = remote(model_half, sib_sum.at[3, pl.ds(2, 2)], fwd_s.at[0], fwd_r.at[0], sibling)
-    forward.start()
-    forward.wait_recv()
-    for block in range(4):
-        mine = model_half[block % 2]
-        theirs = sib_sum[3, 2 + block % 2]
-        set_weights(block, jnp.where(block // 2 == c, mine, theirs))
-
-    for t in range(6):
-        arrived(right_rows.at[t], basis_r.at[0, t])
+    local_model_copy.wait()
+    group_partials(0)
+    pl.semaphore_wait(barrier, 39 - (pair == c).astype(jnp.int32))
+    for index in range(4):
+        send(*group_copy(index))
+    group_partials(1)
+    for index in range(4, 8):
+        send(*group_copy(index))
+    for t in range(2):
         send_basis(1, t)
-        transpose(right_rows, right_cols, t)
-        if t % 3 == 2:
-            partials(0, right_cols, t // 3)
+    for h in range(2):
+        arrived(group_in.at[h], group_r.at[h])
+        total = group_in[h, 0].astype(F32)
+        for g in range(1, 4):
+            total = total + group_in[h, g].astype(F32)
+        fill_outbox(0, h, total)
+        for t in range(2 * h + 2, 2 * h + 4):
+            send_basis(1, t)
+    for l in range(2):
+        send(*init_copies(l)[1])
+    for copy in small:
+        copy.wait()
+
+    mute_t = mute[...].astype(F32).T
+    mute_rows[...] = jnp.concatenate([mute_t, mute_t], 1)
+    first_row = pl.multiple_of(32 * x + 16 * c, 16)
+    window = jnp.where(
+        low, mute_rows[pl.ds(first_row, 8, stride=2), :], mute_rows[pl.ds(first_row + 1, 8, stride=2), :]
+    )
+    cutoff = jnp.concatenate([thresholds[...], thresholds[...]], 1)
+
     for t in range(6):
         arrived(left_rows.at[t], basis_r.at[1, t])
+        send_basis(0, t)
         transpose(left_rows, left_cols, t)
+    for l in range(2):
+        send(*init_copies(l)[0])
     arrived(recorded_half, init_r.at[1])
-    forward.wait_send()
 
     for outer in range(2):
         if outer == 1:
             partials(2, right_cols, 0)
             partials(2, right_cols, 1)
+            send_line(2)
         residual(2 * outer)
         partials(2 * outer + 1, left_cols, 0)
         partials(2 * outer + 1, left_cols, 1)
+        send_line(2 * outer + 1)
         if outer == 1:
             for q in range(2):
                 send(*misfit_copy(q))
+        else:
+            for t in range(6):
+                arrived(right_rows.at[t], basis_r.at[0, t])
+                transpose(right_rows, right_cols, t)
+            arrived(model_half, init_r.at[0])
         update(2 * outer + 1)
         sparsify(outer)
         if outer == 0:
             traces_b[...] = traces[...].astype(BF16)
 
-            def back_one(index, carry):
-                send(*back_copy(index))
-                return carry
-            lax.fori_loop(0, 32, back_one, 0)
+            for index in range(32):
+                send(*back_copy(index), may_be_me=index == 31)
             arrived(model_full, back_r.at[0])
             for block in range(4):
                 set_weights(block, model_full[128 * block:128 * block + 128, :].astype(F32))
@@ -355,6 +437,8 @@
         for item in init_copies(l):
             sent(*item)
         sent(*misfit_copy(l))
+    for index in range(8):
+        sent(*group_copy(index))
     for step in range(4):
         def z_done(s, carry):
             sent(*z_copy(step, s))
@@ -367,16 +451,11 @@
             for q in range(2):
                 exchange(step, 2 * (1 - c) + q, q).wait_send()
 
-    def spread_done(index, carry):
+    for index in range(16):
         for outer in range(2):
-            sent(*spread_copy(outer, index))
-        return carry
-    lax.fori_loop(0, 16, spread_done, 0)
-
-    def back_done(index, carry):
-        sent(*back_copy(index))
-        return carry
-    lax.fori_loop(0, 32, back_done, 0)
+            sent(*spread_copy(outer, index), may_be_me=index >= 14)
+    for index in range(32):
+        sent(*back_copy(index), may_be_me=index == 31)
 
     def final_done(index, carry):
         sent(*final_copy(index))
@@ -392,14 +471,13 @@
 
     wave, wave_back = wave_tables()
     anywhere = pl.BlockSpec(memory_space=pl.ANY)
-    vmem = pl.BlockSpec(memory_space=pltpu.VMEM)
     dma = pltpu.SemaphoreType.DMA
     field = jax.ShapeDtypeStruct((2, 128, 128), F32)
     return pl.pallas_call(
         kernel,
         out_shape=(field, field),
-        in_specs=[anywhere] * 4 + [pl.BlockSpec(memory_space=pltpu.SMEM)] + [vmem] * 4,
-        out_specs=(vmem, vmem),
+        in_specs=[anywhere] * 4 + [pl.BlockSpec(memory_space=pltpu.SMEM)] + [anywhere] * 4,
+        out_specs=(anywhere, anywhere),
         scratch_shapes=[
             pltpu.VMEM((6, 512, 2, 128), BF16),
             pltpu.VMEM((6, 512, 2, 128), BF16),
@@ -422,12 +500,23 @@
             pltpu.VMEM((16, 16, 128), F32),
             pltpu.VMEM((16, 16, 128), BF16),
             pltpu.VMEM((128, 128), F32),
-            dma((2, 24)), dma((2, 6)), dma((4,)), dma((2,)), dma((1,)), dma((1,)),
+            pltpu.VMEM((64, 128), jnp.int32),
+            pltpu.VMEM((1, 64), F32),
+            pltpu.VMEM((NT, 96), BF16),
+            pltpu.VMEM((64, NT), BF16),
+            dma((4,)),
+            pltpu.VMEM((2, 12, 128, 2, 128), BF16),
+            pltpu.VMEM((2, 128, 128), F32),
+            pltpu.VMEM((2, 256, 128), BF16),
+            pltpu.VMEM((2, 2, 2, 384, 128), BF16),
+            pltpu.VMEM((2, 4, 384, 128), BF16),
+            dma((5,)), dma((8,)), dma((2,)),
+            dma((2, 24)), dma((2, 6)), dma((4,)), dma((2,)),
             dma((4, 8)), dma((4, 8)), dma((4, 4)), dma((4, 4)),
             dma((2, 16)), dma((2,)), dma((32,)), dma((1,)), dma((8,)), dma((1,)), dma((2,)), dma((1,)),
         ],
         compiler_params=pltpu.CompilerParams(
-            collective_id=0, has_side_effects=True, vmem_limit_bytes=40 * 1024 * 1024
+            collective_id=0, has_side_effects=True, vmem_limit_bytes=60 * 1024 * 1024
         ),
     )(
         lanes(left_basis), lanes(right_basis), start_model, recorded, tile_ranks,

time: 137 us -> 122 us (0.89)
  Pallas kernels: 126 us -> 118 us
  local copies, waits for them, and re-layouts: 9.63 us -> 3.14 us
    pallas_call x1, Pallas kernels: 126 us -> 118 us  [body(): pl.pallas_call(kernel, out_shape=(field, field), in_specs=[anywhere] * 4...]
    unnamed x20 -> x2, local copies, waits for them, and re-layouts: 9.63 us -> 3.14 us
where the time goes in v2:
time: 122 us
  Pallas kernels  118 us (97%)
  local copies, waits for them, and re-layouts  3.14 us (3%)
    pallas_call x1, Pallas kernels, body(): pl.pallas_call(kernel, out_shape=(field, field), in_specs=[anywhere] * 4...  118 us
    unnamed x2, local copies, waits for them, and re-layouts  3.14 us

profile of v2, /device:TPU:1, one launch (start us, length us, event | category | flops | bytes accessed | tf_op | source)
XLA Modules:
  0.0 121.7 jit_solution(12254812333981824927)
XLA Ops:
  0.6 117.9 %shard_map.104 = (f32[2,128,128]{2,1,0:T(8,128)}, f32[2,128,128]{2,1,0:T(8,128)}) custom-call(bf16[2,128,12,2,128]{4,3,2,1,0:T(2,128)(2,1)} %bitcast.8, bf16[2,128,12,2,128]{4,3,2,1,0:T(2,128)(2,1)} %bitcast.9, f32[2,128,128]{2,1,0:T(8,128)} %model0.1, f32[2,128,128]{2,1,0:T(8,128)} %recorded.1, s32[16,16]{1,0:T(8,128)} %ranks.1, s32[64,128]{1,0:T(8,128)} %bitcast.10, ...), custom_call_target="tpu_custom_call" | custom-call | tf_op jit(solution)/shard_map/pallas_call | solution.py:476
  118.6 1.6 %copy.13 = f32[2,128,128]{2,1,0:T(8,128)} copy(f32[2,128,128]{2,1,0:T(8,128)} %get-tuple-element.4) | data formatting | bytes 262144
  120.2 1.6 %copy.14 = f32[2,128,128]{2,1,0:T(8,128)} copy(f32[2,128,128]{2,1,0:T(8,128)} %get-tuple-element.5) | data formatting | bytes 262144

commit v3 on v2

--- a/solution.py
+++ b/solution.py
@@ -46,9 +46,9 @@
     left_rows, right_rows, left_cols, right_cols,
     model_full, model_half, recorded_half, packed, weights, product,
     outbox, inbox, own_sum, sib_sum, misfit_full,
-    spread_out, spread_in, spread_f32, traces, traces_b, mute_rows,
+    spread_out, spread_in, spread_f32, traces, traces_b, mute_rows, window_rows,
     mute, thresholds, wave, wave_back, small_s,
-    local_rows, local_model, local_weights, group_out, group_in, local_r, group_s, group_r,
+    local_rows, local_model, local_weights, group_out, group_in, local_r, group_s, group_r, heard,
     basis_s, basis_r, init_s, init_r, z_s, z_r, ex_s, ex_r,
     sp_s, sp_r, back_s, back_r, fin_s, fin_r, mis_s, mis_r,
 ):
@@ -112,12 +112,6 @@
         )
     ]
 
-    def greet_line(index, carry):
-        @pl.when(8 * c + index != z)
-        def _():
-            greet((x, pair, 8 * c + index, y))
-        return carry
-
     local_model_copy = pltpu.make_async_copy(model0, local_model, local_r.at[4])
     local_model_copy.start()
 
@@ -132,11 +126,21 @@
 
     local_load(0)
     local_load(1)
-    lax.fori_loop(0, 8, greet_line, 0)
-    for dx, dy in PLANE:
+    for dx, dz, dy in ((0, 0, 2), (0, 1, 0), (0, 15, 0), (1, 0, 0), (3, 0, 0), (0, 0, 1), (0, 0, 3), (0, 0, 0)):
         for dc in (1, 0):
-            if (dx, dy, dc) != (0, 0, 0):
-                greet(((x + dx) % 4, (c + dc) % 2, z, (y + dy) % 4))
+            if (dx, dz, dy, dc) != (0, 0, 0, 0):
+                greet(((x + dx) % 4, (c + dc) % 2, (z + dz) % 16, (y + dy) % 4))
+
+    def tell(index, steps):
+        for dx, dz in steps:
+            pl.semaphore_signal(
+                heard.at[index], inc=1, device_id=address(((x + dx) % 4, c, (z + dz) % 16, y)),
+                device_id_type=pl.DeviceIdType.MESH,
+            )
+
+    def hear(index):
+        pl.semaphore_wait(heard.at[index], 2)
+
     for copy in small:
         copy.start()
 
@@ -216,12 +220,14 @@
             if h == 0:
                 local_weights[l] = interleave(local_model[l])
             view = local_rows.reshape(2, 12, 256, 128)
-            for side in range(2):
-                for t3 in range(3):
-                    group_out[h, l, side, 128 * t3:128 * t3 + 128, :] = lax.dot_general(
-                        view[l, 3 * (2 * h + side) + t3], local_weights[l],
-                        (((0,), (0,)), ((), ())), preferred_element_type=F32,
-                    ).astype(BF16)
+            def one_block(index, carry):
+                rows = pl.ds(pl.multiple_of(128 * (index % 3), 128), 128)
+                group_out[h, l, index // 3, rows, :] = lax.dot_general(
+                    view[l, 6 * h + index], local_weights[l],
+                    (((0,), (0,)), ((), ())), preferred_element_type=F32,
+                ).astype(BF16)
+                return carry
+            lax.fori_loop(0, 6, one_block, 0)
 
     def send_line(step):
         place = z % 8
@@ -237,7 +243,7 @@
             send(*z_copy(step, s), may_be_me=k == 7)
 
     def transpose(rows, cols, t):
-        cols[128 * t:128 * t + 128, :] = rows.reshape(6, 1024, 128)[t].T
+        cols[pl.ds(pl.multiple_of(128 * t, 128), 128), :] = rows.reshape(6, 1024, 128)[t].T
 
     def expand(rows, step, block):
         start = 256 * block if isinstance(block, int) else pl.multiple_of(256 * block, 256)
@@ -261,11 +267,13 @@
 
     def residual(step):
         receive_line(step)
-        for block in range(4):
+        def one_sum(block, carry):
             part = expand(left_rows, step, block)
             kept = jnp.where(block // 2 == c, recorded_half[block % 2], 0.0)
             own_sum[step, block] = part - kept
             exchange(step, block, block).start()
+            return carry
+        lax.fori_loop(0, 4, one_sum, 0)
         for block in range(4):
             exchange(step, block, block).wait_recv()
             values = own_sum[step, block] + sib_sum[step, block]
@@ -275,12 +283,17 @@
 
     def update(step):
         receive_line(step)
-        for q in range(2):
-            block = 2 * (1 - c) + q
+        def one_sum(index, carry):
+            block = (2 * (1 - c) + index) % 4
             own_sum[step, block] = expand(right_rows, step, block)
-            exchange(step, block, q).start()
-        for q in range(2):
-            own_sum[step, 2 * c + q] = expand(right_rows, step, 2 * c + q)
+
+            @pl.when(index < 2)
+            def _():
+                exchange(step, block, index % 2).start()
+            return carry
+        lax.fori_loop(0, 4, one_sum, 0)
+        if step == 1:
+            arrived(model_half, init_r.at[0])
         for q in range(2):
             exchange(step, 2 * (1 - c) + q, q).wait_recv()
             total = own_sum[step, 2 * c + q] + sib_sum[step, q]
@@ -307,7 +320,8 @@
         spread_f32[...] = spread_in[outer].reshape(256, 128).astype(F32)
         flat = traces.reshape(256, 128)
         sample = lax.broadcasted_iota(jnp.int32, (NT, 128), 0).astype(F32)
-        for p in range(8):
+
+        def one_pair(p, carry):
             even = spread_f32[pl.ds(2 * p, 16, stride=16), :]
             odd = spread_f32[pl.ds(2 * p + 1, 16, stride=16), :]
             real = jnp.where(low, even, pltpu.roll(odd, 64, 1))
@@ -316,7 +330,7 @@
             series = jnp.dot(
                 wave[...], jnp.concatenate([both, both, both], 0), preferred_element_type=F32
             ) * (1.0 / math.sqrt(NF))
-            series = jnp.where(sample >= window[p:p + 1, :], series, 0.0)
+            series = jnp.where(sample >= window_rows[pl.ds(p, 1), :], series, 0.0)
             series = series - jnp.clip(series, -cutoff, cutoff)
             high = series.astype(BF16)
             rest = (series - high.astype(F32)).astype(BF16)
@@ -326,6 +340,8 @@
             real, imag = returned[0:16], returned[16:32]
             flat[pl.ds(2 * p, 16, stride=16), :] = jnp.where(low, real, pltpu.roll(imag, 64, 1))
             flat[pl.ds(2 * p + 1, 16, stride=16), :] = jnp.where(low, pltpu.roll(real, 64, 1), imag)
+            return carry
+        lax.fori_loop(0, 8, one_pair, 0)
 
     BACK = [(dx, dy, dc) for dx, dy in PLANE for dc in (1, 0)]
 
@@ -355,14 +371,24 @@
 
     local_model_copy.wait()
     group_partials(0)
-    pl.semaphore_wait(barrier, 39 - (pair == c).astype(jnp.int32))
+    pl.semaphore_wait(barrier, 15)
     for index in range(4):
         send(*group_copy(index))
+    tell(0, ((0, 1), (0, 15)))
+    tell(3, ((1, 0), (3, 0)))
     group_partials(1)
     for index in range(4, 8):
         send(*group_copy(index))
     for t in range(2):
         send_basis(1, t)
+    hear(0)
+    tell(1, ((0, 2), (0, 14)))
+    hear(1)
+    tell(2, ((0, 4), (0, 12)))
+    hear(3)
+    tell(4, ((1, 0), (3, 0)))
+    hear(2)
+    hear(4)
     for h in range(2):
         arrived(group_in.at[h], group_r.at[h])
         total = group_in[h, 0].astype(F32)
@@ -379,15 +405,17 @@
     mute_t = mute[...].astype(F32).T
     mute_rows[...] = jnp.concatenate([mute_t, mute_t], 1)
     first_row = pl.multiple_of(32 * x + 16 * c, 16)
-    window = jnp.where(
+    window_rows[...] = jnp.where(
         low, mute_rows[pl.ds(first_row, 8, stride=2), :], mute_rows[pl.ds(first_row + 1, 8, stride=2), :]
     )
     cutoff = jnp.concatenate([thresholds[...], thresholds[...]], 1)
 
-    for t in range(6):
+    def left_block(t, carry):
         arrived(left_rows.at[t], basis_r.at[1, t])
         send_basis(0, t)
         transpose(left_rows, left_cols, t)
+        return carry
+    lax.fori_loop(0, 6, left_block, 0)
     for l in range(2):
         send(*init_copies(l)[0])
     arrived(recorded_half, init_r.at[1])
@@ -405,10 +433,11 @@
             for q in range(2):
                 send(*misfit_copy(q))
         else:
-            for t in range(6):
+            def right_block(t, carry):
                 arrived(right_rows.at[t], basis_r.at[0, t])
                 transpose(right_rows, right_cols, t)
-            arrived(model_half, init_r.at[0])
+                return carry
+            lax.fori_loop(0, 6, right_block, 0)
         update(2 * outer + 1)
         sparsify(outer)
         if outer == 0:
@@ -500,6 +529,7 @@
             pltpu.VMEM((16, 16, 128), F32),
             pltpu.VMEM((16, 16, 128), BF16),
             pltpu.VMEM((128, 128), F32),
+            pltpu.VMEM((8, 128), F32),
             pltpu.VMEM((64, 128), jnp.int32),
             pltpu.VMEM((1, 64), F32),
             pltpu.VMEM((NT, 96), BF16),
@@ -510,7 +540,7 @@
             pltpu.VMEM((2, 256, 128), BF16),
             pltpu.VMEM((2, 2, 2, 384, 128), BF16),
             pltpu.VMEM((2, 4, 384, 128), BF16),
-            dma((5,)), dma((8,)), dma((2,)),
+            dma((5,)), dma((8,)), dma((2,)), pltpu.SemaphoreType.REGULAR((5,)),
             dma((2, 24)), dma((2, 6)), dma((4,)), dma((2,)),
             dma((4, 8)), dma((4, 8)), dma((4, 4)), dma((4, 4)),
             dma((2, 16)), dma((2,)), dma((32,)), dma((1,)), dma((8,)), dma((1,)), dma((2,)), dma((1,)),

time: 122 us -> 125 us (1.025)
  Pallas kernels: 118 us -> 121 us
    pallas_call x1, Pallas kernels: 118 us -> 121 us  [body(): pl.pallas_call(kernel, out_shape=(field, field), in_specs=[anywhere] * 4...]
where the time goes in v3:
time: 125 us; the launch traced here: 124 us
  Pallas kernels  121 us (97%)
  local copies, waits for them, and re-layouts  3.14 us (3%)
    pallas_call x1, Pallas kernels, body(): pl.pallas_call(kernel, out_shape=(field, field), in_specs=[anywhere] * 4...  121 us
    unnamed x2, local copies, waits for them, and re-layouts  3.14 us

profile of v3, /device:TPU:1, one launch (start us, length us, event | category | flops | bytes accessed | tf_op | source)
XLA Modules:
  0.0 124.3 jit_solution(16822479388445381486)
XLA Ops:
  0.6 120.6 %shard_map.104 = (f32[2,128,128]{2,1,0:T(8,128)}, f32[2,128,128]{2,1,0:T(8,128)}) custom-call(bf16[2,128,12,2,128]{4,3,2,1,0:T(2,128)(2,1)} %bitcast.8, bf16[2,128,12,2,128]{4,3,2,1,0:T(2,128)(2,1)} %bitcast.9, f32[2,128,128]{2,1,0:T(8,128)} %model0.1, f32[2,128,128]{2,1,0:T(8,128)} %recorded.1, s32[16,16]{1,0:T(8,128)} %ranks.1, s32[64,128]{1,0:T(8,128)} %bitcast.10, ...), custom_call_target="tpu_custom_call" | custom-call | tf_op jit(solution)/shard_map/pallas_call | solution.py:505
  121.2 1.6 %copy.13 = f32[2,128,128]{2,1,0:T(8,128)} copy(f32[2,128,128]{2,1,0:T(8,128)} %get-tuple-element.4) | data formatting | bytes 262144
  122.8 1.6 %copy.14 = f32[2,128,128]{2,1,0:T(8,128)} copy(f32[2,128,128]{2,1,0:T(8,128)} %get-tuple-element.5) | data formatting | bytes 262144

commit v4 on v3

--- a/solution.py
+++ b/solution.py
@@ -227,7 +227,8 @@
                     (((0,), (0,)), ((), ())), preferred_element_type=F32,
                 ).astype(BF16)
                 return carry
-            lax.fori_loop(0, 6, one_block, 0)
+            for index in range(6):
+                one_block(index, 0)
 
     def send_line(step):
         place = z % 8
@@ -267,13 +268,11 @@
 
     def residual(step):
         receive_line(step)
-        def one_sum(block, carry):
+        for block in range(4):
             part = expand(left_rows, step, block)
             kept = jnp.where(block // 2 == c, recorded_half[block % 2], 0.0)
             own_sum[step, block] = part - kept
             exchange(step, block, block).start()
-            return carry
-        lax.fori_loop(0, 4, one_sum, 0)
         for block in range(4):
             exchange(step, block, block).wait_recv()
             values = own_sum[step, block] + sib_sum[step, block]
@@ -283,15 +282,12 @@
 
     def update(step):
         receive_line(step)
-        def one_sum(index, carry):
-            block = (2 * (1 - c) + index) % 4
+        for q in range(2):
+            block = 2 * (1 - c) + q
             own_sum[step, block] = expand(right_rows, step, block)
-
-            @pl.when(index < 2)
-            def _():
-                exchange(step, block, index % 2).start()
-            return carry
-        lax.fori_loop(0, 4, one_sum, 0)
+            exchange(step, block, q).start()
+        for q in range(2):
+            own_sum[step, 2 * c + q] = expand(right_rows, step, 2 * c + q)
         if step == 1:
             arrived(model_half, init_r.at[0])
         for q in range(2):
@@ -330,7 +326,7 @@
             series = jnp.dot(
                 wave[...], jnp.concatenate([both, both, both], 0), preferred_element_type=F32
             ) * (1.0 / math.sqrt(NF))
-            series = jnp.where(sample >= window_rows[pl.ds(p, 1), :], series, 0.0)
+            series = jnp.where(sample >= window_rows[p:p + 1, :], series, 0.0)
             series = series - jnp.clip(series, -cutoff, cutoff)
             high = series.astype(BF16)
             rest = (series - high.astype(F32)).astype(BF16)
@@ -341,7 +337,8 @@
             flat[pl.ds(2 * p, 16, stride=16), :] = jnp.where(low, real, pltpu.roll(imag, 64, 1))
             flat[pl.ds(2 * p + 1, 16, stride=16), :] = jnp.where(low, pltpu.roll(real, 64, 1), imag)
             return carry
-        lax.fori_loop(0, 8, one_pair, 0)
+        for p in range(8):
+            one_pair(p, 0)
 
     BACK = [(dx, dy, dc) for dx, dy in PLANE for dc in (1, 0)]
 

time: 125 us -> 118 us (0.944)
  Pallas kernels: 121 us -> 114 us
    pallas_call x1, Pallas kernels: 121 us -> 114 us  [body(): pl.pallas_call(kernel, out_shape=(field, field), in_specs=[anywhere] * 4...]
where the time goes in v4:
time: 118 us
  Pallas kernels  114 us (97%)
  local copies, waits for them, and re-layouts  3.14 us (3%)
    pallas_call x1, Pallas kernels, body(): pl.pallas_call(kernel, out_shape=(field, field), in_specs=[anywhere] * 4...  114 us
    unnamed x2, local copies, waits for them, and re-layouts  3.14 us

profile of v4, /device:TPU:1, one launch (start us, length us, event | category | flops | bytes accessed | tf_op | source)
XLA Modules:
  0.0 117.9 jit_solution(7350480174898591576)
XLA Ops:
  0.6 114.1 %shard_map.104 = (f32[2,128,128]{2,1,0:T(8,128)}, f32[2,128,128]{2,1,0:T(8,128)}) custom-call(bf16[2,128,12,2,128]{4,3,2,1,0:T(2,128)(2,1)} %bitcast.8, bf16[2,128,12,2,128]{4,3,2,1,0:T(2,128)(2,1)} %bitcast.9, f32[2,128,128]{2,1,0:T(8,128)} %model0.1, f32[2,128,128]{2,1,0:T(8,128)} %recorded.1, s32[16,16]{1,0:T(8,128)} %ranks.1, s32[64,128]{1,0:T(8,128)} %bitcast.10, ...), custom_call_target="tpu_custom_call" | custom-call | tf_op jit(solution)/shard_map/pallas_call | solution.py:502
  114.7 1.6 %copy.13 = f32[2,128,128]{2,1,0:T(8,128)} copy(f32[2,128,128]{2,1,0:T(8,128)} %get-tuple-element.4) | data formatting | bytes 262144
  116.3 1.6 %copy.14 = f32[2,128,128]{2,1,0:T(8,128)} copy(f32[2,128,128]{2,1,0:T(8,128)} %get-tuple-element.5) | data formatting | bytes 262144

commit v5 on v4

--- a/solution.py
+++ b/solution.py
@@ -174,14 +174,15 @@
     low = lane < 64
     sign = jnp.where(low, 1.0, -1.0).astype(F32)
 
-    def interleave(values):
+    def interleave(values, slot):
         values = values.astype(BF16).astype(F32)
-        packed[pl.ds(0, 128, stride=2), :] = values
-        packed[pl.ds(1, 128, stride=2), :] = pltpu.roll(values, 64, 1) * sign
-        return packed[...].astype(BF16)
+        flat = packed.reshape(1024, 128)
+        flat[pl.ds(256 * slot, 128, stride=2), :] = values
+        flat[pl.ds(256 * slot + 1, 128, stride=2), :] = pltpu.roll(values, 64, 1) * sign
+        return flat[256 * slot:256 * slot + 256, :].astype(BF16)
 
     def set_weights(block, values):
-        weights[256 * block:256 * block + 256, :] = interleave(values)
+        weights[256 * block:256 * block + 256, :] = interleave(values, block)
 
     slots = lax.broadcasted_iota(jnp.int32, (96, 128), 0)
 
@@ -218,7 +219,7 @@
         for l in range(2):
             arrived(local_rows.at[l, pl.ds(6 * h, 6)], local_r.at[2 * h + l])
             if h == 0:
-                local_weights[l] = interleave(local_model[l])
+                local_weights[l] = interleave(local_model[l], l)
             view = local_rows.reshape(2, 12, 256, 128)
             def one_block(index, carry):
                 rows = pl.ds(pl.multiple_of(128 * (index % 3), 128), 128)
@@ -246,14 +247,15 @@
     def transpose(rows, cols, t):
         cols[pl.ds(pl.multiple_of(128 * t, 128), 128), :] = rows.reshape(6, 1024, 128)[t].T
 
-    def expand(rows, step, block):
+    def expand(rows, step, block, slot):
         start = 256 * block if isinstance(block, int) else pl.multiple_of(256 * block, 256)
         view = rows.reshape(6, 1024, 128)
         lhs = jnp.concatenate([view[t, pl.ds(start, 256), :] for t in range(6)], 1)
         rhs = inbox[step].reshape(768, 128)
-        product[...] = jnp.dot(lhs, rhs, preferred_element_type=F32)
-        real = product[pl.ds(0, 128, stride=2), :]
-        imag = product[pl.ds(1, 128, stride=2), :]
+        flat = product.reshape(1024, 128)
+        flat[256 * slot:256 * slot + 256, :] = jnp.dot(lhs, rhs, preferred_element_type=F32)
+        real = flat[pl.ds(256 * slot, 128, stride=2), :]
+        imag = flat[pl.ds(256 * slot + 1, 128, stride=2), :]
         return real - pltpu.roll(imag, 64, 1) * sign
 
     def exchange(step, block, slot):
@@ -269,7 +271,7 @@
     def residual(step):
         receive_line(step)
         for block in range(4):
-            part = expand(left_rows, step, block)
+            part = expand(left_rows, step, block, block)
             kept = jnp.where(block // 2 == c, recorded_half[block % 2], 0.0)
             own_sum[step, block] = part - kept
             exchange(step, block, block).start()
@@ -284,10 +286,10 @@
         receive_line(step)
         for q in range(2):
             block = 2 * (1 - c) + q
-            own_sum[step, block] = expand(right_rows, step, block)
+            own_sum[step, block] = expand(right_rows, step, block, q)
             exchange(step, block, q).start()
         for q in range(2):
-            own_sum[step, 2 * c + q] = expand(right_rows, step, 2 * c + q)
+            own_sum[step, 2 * c + q] = expand(right_rows, step, 2 * c + q, 2 + q)
         if step == 1:
             arrived(model_half, init_r.at[0])
         for q in range(2):
@@ -512,9 +514,9 @@
             pltpu.VMEM((512, 128), BF16),
             pltpu.VMEM((2, 128, 128), F32),
             pltpu.VMEM((2, 128, 128), F32),
-            pltpu.VMEM((256, 128), F32),
+            pltpu.VMEM((4, 256, 128), F32),
             pltpu.VMEM((1024, 128), BF16),
-            pltpu.VMEM((256, 128), F32),
+            pltpu.VMEM((4, 256, 128), F32),
             pltpu.VMEM((4, 8, 96, 128), BF16),
             pltpu.VMEM((4, 8, 96, 128), BF16),
             pltpu.VMEM((4, 4, 128, 128), F32),

time: 118 us -> 118 us (level)
  no operation moved by 1% of the time
where the time goes in v5:
time: 118 us
  Pallas kernels  114 us (97%)
  local copies, waits for them, and re-layouts  3.14 us (3%)
    pallas_call x1, Pallas kernels, body(): pl.pallas_call(kernel, out_shape=(field, field), in_specs=[anywhere] * 4...  114 us
    unnamed x2, local copies, waits for them, and re-layouts  3.14 us

profile of v5, /device:TPU:1, one launch (start us, length us, event | category | flops | bytes accessed | tf_op | source)
XLA Modules:
  0.0 117.9 jit_solution(3681753035329810964)
XLA Ops:
  0.6 114.1 %shard_map.104 = (f32[2,128,128]{2,1,0:T(8,128)}, f32[2,128,128]{2,1,0:T(8,128)}) custom-call(bf16[2,128,12,2,128]{4,3,2,1,0:T(2,128)(2,1)} %bitcast.8, bf16[2,128,12,2,128]{4,3,2,1,0:T(2,128)(2,1)} %bitcast.9, f32[2,128,128]{2,1,0:T(8,128)} %model0.1, f32[2,128,128]{2,1,0:T(8,128)} %recorded.1, s32[16,16]{1,0:T(8,128)} %ranks.1, s32[64,128]{1,0:T(8,128)} %bitcast.10, ...), custom_call_target="tpu_custom_call" | custom-call | tf_op jit(solution)/shard_map/pallas_call | solution.py:504
  114.8 1.6 %copy.13 = f32[2,128,128]{2,1,0:T(8,128)} copy(f32[2,128,128]{2,1,0:T(8,128)} %get-tuple-element.4) | data formatting | bytes 262144
  116.3 1.6 %copy.14 = f32[2,128,128]{2,1,0:T(8,128)} copy(f32[2,128,128]{2,1,0:T(8,128)} %get-tuple-element.5) | data formatting | bytes 262144
